TPU v7x, 32 devices: a whole 2x2x4 slice. The times are simulated.
32 devices in a mesh: rows: 8 (over z, y), cols: 4 (over x, core).
Axes of the slice: x: 2, y: 2, z: 4, core: 2. Of those that a mesh axis runs over, the one named last changes fastest.
Arguments:
- tile_blocks: bfloat16 [256, 8, 256, 256], P(('rows', 'cols')), may hold values from 0.049804688 to 1
- tile_cols: int32 [256, 8], P(('rows', 'cols')), may hold values from 0 to 255, as said below
- tile_count: int32 [256], P(('rows', 'cols')), may hold values from 1 to 8
- start_mass: float32 [65536], P(('rows', 'cols')), may hold values from 0.5 to 64
- probe_block: bfloat16 [32, 65536], P(None, ('rows', 'cols')), may hold values from -6 to 6
Outputs:
- basis: float32 [32, 65536], P(None, ('rows', 'cols'))
Inputs may be any that keep to these rules, and one draw needn't show every extreme that they name: `tile_cols`: slot 0 names the block row itself; every other slot names a block within 8 blocks of its row, cyclically over 256.
All inputs are finite; a program needn't handle non-finite values.
Results may differ from a plain program's by a relative error of at most 0.00035.
The roundings to bfloat16 on the way count: a program that leaves them out, or rounds other values in their place, can miss the bound.
Values may be sent and summed in bfloat16 or wider, within the bound.
A program may use at most 64 MiB of HBM per device.

v0:
```python
import math

import jax
import jax.numpy as jnp
from jax import lax
from jax.sharding import PartitionSpec as P

POWER = 4


def shifted(shard, axis, by):
    devices = lax.axis_size(axis)
    return lax.ppermute(shard, axis, [(i, (i + by) % devices) for i in range(devices)])


def with_halo(block, sides, width):
    for axis, dim in sides:
        count = lax.axis_size(axis)
        forward = [(i, i + 1) for i in range(count - 1)]
        forward.append((count - 1, 0))
        backward = [(target, source) for source, target in forward]
        low = lax.ppermute(
            lax.slice_in_dim(block, block.shape[dim] - width, None, axis=dim), axis, forward
        )
        high = lax.ppermute(lax.slice_in_dim(block, 0, width, axis=dim), axis, backward)
        block = jnp.concatenate([low, block, high], axis=dim)
    return block


def spread_rows(tile_blocks, weighted, place_table):
    chans = weighted.shape[0]
    blocks_dev, slot_count, tile_width = (
        tile_blocks.shape[0],
        tile_blocks.shape[1],
        tile_blocks.shape[2],
    )
    contrib = jnp.einsum(
        "bkij,cbi->cbkj", tile_blocks, weighted, preferred_element_type=jnp.float32
    )
    contrib = contrib.reshape(chans, blocks_dev * slot_count, tile_width)
    return jnp.einsum("wm,cmj->cwj", place_table, contrib, precision=lax.Precision.HIGHEST)


def per_device(tile_blocks, tile_cols, tile_count, start_mass, probe_block):
    blocks_dev, slot_count, tile_width = (
        tile_blocks.shape[0],
        tile_blocks.shape[1],
        tile_blocks.shape[2],
    )
    chans = probe_block.shape[0]
    devices = lax.axis_size(("rows", "cols"))
    total_blocks = blocks_dev * devices
    zone_root = math.sqrt(total_blocks * tile_width)
    first_block = lax.axis_index(("rows", "cols")) * blocks_dev
    live_slots = (jnp.arange(slot_count)[None, :] < tile_count[:, None]).astype(jnp.float32)
    local_index = (tile_cols - first_block + blocks_dev) % total_blocks
    place_table = (jnp.arange(3 * blocks_dev)[:, None] == local_index.reshape(-1)[None, :]).astype(
        jnp.float32
    )
    place_table = place_table * live_slots.reshape(-1)[None, :]
    partial_rows = jnp.sum(tile_blocks, axis=3, dtype=jnp.float32)
    row_sum = jnp.sum(partial_rows * live_slots[:, :, None], axis=1)
    row_inverse = 1.0 / row_sum
    stationary = start_mass.reshape(blocks_dev, tile_width)
    for power_step in range(POWER):
        weighted = (stationary * row_inverse).astype(jnp.bfloat16)
        window = spread_rows(tile_blocks, weighted[None], place_table)[0]
        lower_part = window[:blocks_dev]
        middle_part = window[blocks_dev : 2 * blocks_dev]
        upper_part = window[2 * blocks_dev :]
        arrived = middle_part + shifted(upper_part, ("rows", "cols"), 1)
        arrived = arrived + shifted(lower_part, ("rows", "cols"), -1)
        raw_mass = 0.85 * arrived + 0.15
        square_total = lax.psum(jnp.sum(raw_mass * raw_mass), ("rows", "cols"))
        stationary = raw_mass * zone_root / jnp.sqrt(square_total)
    root_mass = jnp.sqrt(stationary)
    probe_rows = probe_block.reshape(chans, blocks_dev, tile_width).astype(jnp.float32)
    plain_window = with_halo(probe_block, ((("rows", "cols"), 1),), blocks_dev * tile_width)
    root_window = with_halo(
        root_mass.reshape(-1), ((("rows", "cols"), 0),), blocks_dev * tile_width
    )
    probe_window = (plain_window.astype(jnp.float32) / root_window[None, :]).astype(jnp.bfloat16)
    probe_window = probe_window.reshape(chans, 3 * blocks_dev, tile_width)
    gathered = probe_window[:, local_index] * live_slots.astype(jnp.bfloat16)[None, :, :, None]
    forward_term = jnp.einsum(
        "bkij,cbkj->cbi", tile_blocks, gathered, preferred_element_type=jnp.float32
    )
    forward_term = forward_term * (root_mass * row_inverse)[None]
    pushed = (probe_rows * (root_mass * row_inverse)[None]).astype(jnp.bfloat16)
    window = spread_rows(tile_blocks, pushed, place_table)
    lower_part = window[:, :blocks_dev]
    middle_part = window[:, blocks_dev : 2 * blocks_dev]
    upper_part = window[:, 2 * blocks_dev :]
    landed = middle_part + shifted(upper_part, ("rows", "cols"), 1)
    landed = landed + shifted(lower_part, ("rows", "cols"), -1)
    transposed_term = landed / root_mass[None]
    embedded = (0.5 * (forward_term + transposed_term)).reshape(chans, blocks_dev * tile_width)
    gram_matrix = lax.psum(
        jnp.dot(embedded, embedded.T, precision=lax.Precision.HIGHEST), ("rows", "cols")
    )
    lower_factor = jnp.linalg.cholesky(gram_matrix)
    return jax.scipy.linalg.solve_triangular(lower_factor, embedded, lower=True)


def solution(mesh):
    return jax.shard_map(
        per_device,
        mesh=mesh,
        in_specs=(
            P(("rows", "cols"), None, None, None),
            P(("rows", "cols"), None),
            P(("rows", "cols")),
            P(("rows", "cols")),
            P(None, ("rows", "cols")),
        ),
        out_specs=P(None, ("rows", "cols")),
        check_vma=False,
    )
```

profile of v0, /device:TPU:0, one launch (start us, length us, event | category | flops | bytes accessed | tf_op | source)
XLA Modules:
  0.0 290.5 jit_solution(7868933309512952568)
XLA Ops:
  0.0 0.7 compare_select_fusion
  0.7 0.1 eq.18
  0.8 0.7 fusion.77
  1.5 5.6 %convert_reduce_fusion = f32[8,8,256]{2,1,0:T(8,128)S(1)} fusion(bf16[8,8,256,256]{3,2,1,0:T(8,128)(2,1)} %param.5), kind=kLoop, calls=%fused_computation.1 | loop fusion | flops 8372224 | bytes 8454144 | tf_op jit(solution)/shard_map/reduce_sum | solution.py:61
  7.2 0.1 multiply_reduce_fusion
  7.4 4.6 %fusion.54 = f32[8,1,8,256]{3,1,2,0:T(1,128)S(1)} fusion(bf16[8,8,256,256]{3,2,1,0:T(8,128)(2,1)} %param.5, bf16[8,256,1,1]{1,0,2,3:T(8,128)(2,1)S(1)} %fusion.72), kind=kOutput, calls=%fused_computation.89 | convolution fusion | flops 8388608 | bytes 8458240 | tf_op jit(solution)/shard_map/bkij,cbi->cbkj/dot_general | solution.py:37
  11.9 0.2 convolution_bitcast_fusion.4
  12.1 0.5 collective-permute-start.2
  12.6 6.0 %collective-permute-start.3 = (f32[8,256]{1,0:T(8,128)S(1)}, f32[8,256]{1,0:T(8,128)S(1)}, u32[]{:S(2)}, u32[]{:S(2)}) collective-permute-start(f32[8,256]{1,0:T(8,128)S(1)} %get-tuple-element.18), channel_id=1, source_target_pairs={{0,31},{1,0},{2,1},{3,2},{4,3},{5,4},{6,5},{7,6},{8,7},{9,8},{10,9... | collective-permute-start | bytes 24584 | tf_op jit(solution)/shard_map/ppermute | solution.py:13
  18.6 1.3 collective-permute-done.2
  19.9 0.1 collective-permute-done.3
  20.0 0.6 multiply_reduce_fusion.4
  20.6 38.9 %psum.35 = f32[]{:T(128)} all-reduce(f32[]{:T(128)} %multiply_reduce_fusion.4), channel_id=1, replica_groups=mesh['rows'=8,'cols'=4] {'rows','cols'}, use_global_device_ids=true, to_apply=%region_3.4 | all-reduce | flops 1 | bytes 8 | tf_op jit(solution)/shard_map/psum | solution.py:74
  60.3 4.6 %fusion.52 = f32[8,1,8,256]{3,1,2,0:T(1,128)S(1)} fusion(bf16[8,8,256,256]{3,2,1,0:T(8,128)(2,1)} %param.5, bf16[8,256,1,1]{1,0,2,3:T(8,128)(2,1)S(1)} %fusion.73), kind=kOutput, calls=%fused_computation.87 | convolution fusion | flops 8388608 | bytes 8458240 | tf_op jit(solution)/shard_map/bkij,cbi->cbkj/dot_general | solution.py:37
  64.9 0.2 convolution_bitcast_fusion.3
  65.1 5.3 %collective-permute-start.5 = (f32[8,256]{1,0:T(8,128)S(1)}, f32[8,256]{1,0:T(8,128)S(1)}, u32[]{:S(2)}, u32[]{:S(2)}) collective-permute-start(f32[8,256]{1,0:T(8,128)S(1)} %get-tuple-element.16), channel_id=1, source_target_pairs={{0,31},{1,0},{2,1},{3,2},{4,3},{5,4},{6,5},{7,6},{8,7},{9,8},{10,9... | collective-permute-start | bytes 24584 | tf_op jit(solution)/shard_map/ppermute | solution.py:13
  70.4 1.3 collective-permute-done.4
  71.8 0.6 multiply_reduce_fusion.3
  72.4 38.8 %psum.36 = f32[]{:T(128)} all-reduce(f32[]{:T(128)} %multiply_reduce_fusion.3), channel_id=1, replica_groups=mesh['rows'=8,'cols'=4] {'rows','cols'}, use_global_device_ids=true, to_apply=%region_5.6 | all-reduce | flops 1 | bytes 8 | tf_op jit(solution)/shard_map/psum | solution.py:74
  111.9 4.6 %fusion.50 = f32[8,1,8,256]{3,1,2,0:T(1,128)S(1)} fusion(bf16[8,8,256,256]{3,2,1,0:T(8,128)(2,1)} %param.5, bf16[8,256,1,1]{1,0,2,3:T(8,128)(2,1)S(1)} %fusion.74), kind=kOutput, calls=%fused_computation.85 | convolution fusion | flops 8388608 | bytes 8458240 | tf_op jit(solution)/shard_map/bkij,cbi->cbkj/dot_general | solution.py:37
  116.5 0.2 convolution_bitcast_fusion.2
  116.7 5.3 %collective-permute-start.7 = (f32[8,256]{1,0:T(8,128)S(1)}, f32[8,256]{1,0:T(8,128)S(1)}, u32[]{:S(2)}, u32[]{:S(2)}) collective-permute-start(f32[8,256]{1,0:T(8,128)S(1)} %get-tuple-element.14), channel_id=1, source_target_pairs={{0,31},{1,0},{2,1},{3,2},{4,3},{5,4},{6,5},{7,6},{8,7},{9,8},{10,9... | collective-permute-start | bytes 24584 | tf_op jit(solution)/shard_map/ppermute | solution.py:13
  122.1 0.5 collective-permute-start
  122.6 0.8 collective-permute-done.6
  123.4 0.6 multiply_reduce_fusion.2
  124.1 39.0 %psum.37 = f32[]{:T(128)} all-reduce(f32[]{:T(128)} %multiply_reduce_fusion.2), channel_id=1, replica_groups=mesh['rows'=8,'cols'=4] {'rows','cols'}, use_global_device_ids=true, to_apply=%region_7.8 | all-reduce | flops 1 | bytes 8 | tf_op jit(solution)/shard_map/psum | solution.py:74
  163.8 4.6 %fusion.48 = f32[8,1,8,256]{3,1,2,0:T(1,128)S(1)} fusion(bf16[8,8,256,256]{3,2,1,0:T(8,128)(2,1)} %param.5, bf16[8,256,1,1]{1,0,2,3:T(8,128)(2,1)S(1)} %fusion.75), kind=kOutput, calls=%fused_computation.83 | convolution fusion | flops 8388608 | bytes 8458240 | tf_op jit(solution)/shard_map/bkij,cbi->cbkj/dot_general | solution.py:37
  168.4 0.2 convolution_bitcast_fusion.1
  168.6 5.3 %collective-permute-start.9 = (f32[8,256]{1,0:T(8,128)S(1)}, f32[8,256]{1,0:T(8,128)S(1)}, u32[]{:S(2)}, u32[]{:S(2)}) collective-permute-start(f32[8,256]{1,0:T(8,128)S(1)} %get-tuple-element.12), channel_id=1, source_target_pairs={{0,31},{1,0},{2,1},{3,2},{4,3},{5,4},{6,5},{7,6},{8,7},{9,8},{10,9... | collective-permute-start | bytes 24584 | tf_op jit(solution)/shard_map/ppermute | solution.py:13
  174.0 1.3 collective-permute-done.8
  175.3 0.6 multiply_reduce_fusion.1
  176.0 38.8 %psum.38 = f32[]{:T(128)} all-reduce(f32[]{:T(128)} %multiply_reduce_fusion.1), channel_id=1, replica_groups=mesh['rows'=8,'cols'=4] {'rows','cols'}, use_global_device_ids=true, to_apply=%region_9.10 | all-reduce | flops 1 | bytes 8 | tf_op jit(solution)/shard_map/psum | solution.py:74
  215.6 5.3 %collective-permute-start.11 = (f32[2048]{0:T(1024)S(1)}, f32[2048]{0:T(1024)S(1)}, u32[]{:S(2)}, u32[]{:S(2)}) collective-permute-start(f32[2048]{0:T(1024)S(1)} %bitcast.201), channel_id=1, source_target_pairs={{1,0},{2,1},{3,2},{4,3},{5,4},{6,5},{7,6},{8,7},{9,8},{10,9},{11,1... | collective-permute-start | bytes 24584 | tf_op jit(solution)/shard_map/ppermute | solution.py:25
  221.0 4.8 %fusion.12 = f32[8,32,8,256]{3,1,2,0:T(8,128)S(1)} fusion(bf16[8,8,256,256]{3,2,1,0:T(8,128)(2,1)} %param.5, bf16[32,8,256,1]{2,1,0,3:T(8,128)(2,1)S(1)} %fusion.11), kind=kOutput, calls=%fused_computation.27 | convolution fusion | flops 268435456 | bytes 10616832 | tf_op jit(solution)/shard_map/bkij,cbi->cbkj/dot_general | solution.py:37
  225.8 2.4 fusion
  228.2 0.3 copy.87
  228.6 5.3 %collective-permute-start.13 = (f32[32,8,256]{2,0,1:T(8,128)S(1)}, f32[32,8,256]{2,0,1:T(8,128)S(1)}, u32[]{:S(2)}, u32[]{:S(2)}) collective-permute-start(f32[32,8,256]{2,0,1:T(8,128)S(1)} %get-tuple-element.10), channel_id=1, source_target_pairs={{0,31},{1,0},{2,1},{3,2},{4,3},{5,4},{6,5},{7,6},{8,7},{9,8},{10,9... | collective-permute-start | bytes 786440 | tf_op jit(solution)/shard_map/ppermute | solution.py:13
  234.0 0.1 divide_convert_fusion
  234.1 0.6 gather_fusion
  234.7 3.2 %collective-permute-done.12 = f32[32,8,256]{2,0,1:T(8,128)S(1)} collective-permute-done((f32[32,8,256]{2,0,1:T(8,128)S(1)}, f32[32,8,256]{2,0,1:T(8,128)S(1)}, u32[]{:S(2)}, u32[]{:S(2)}) %collective-permute-start.12) | collective-permute-done | bytes 262176 | tf_op jit(solution)/shard_map/ppermute | solution.py:13
  237.9 5.9 %fusion.10 = f32[32,8,256]{2,0,1:T(8,128)S(1)} fusion(f32[32,8,256]{2,0,1:T(8,128)S(1)} %collective-permute-done.13, f32[32,8,256]{2,0,1:T(8,128)S(1)} %collective-permute-done.12, f32[32,24,256]{2,0,1:T(8,128)S(1)} %bitcast.190, f32[8,256]{1,0:T(8,128)S(1)} %get-tuple-element.8, f32[8,256]{1,0:T(8,128)S(1)} %get-tuple-element.7, ...), kind=kOutput, calls=%fused_computation.21 | convolution fusion | flops 269352960 | bytes 10502272 | tf_op jit(solution)/shard_map/bkij,cbkj->cbi/dot_general | solution.py:85
  243.9 0.3 convolution_bitcast_fusion.5
  244.3 38.3 %psum.39 = f32[32,32]{0,1:T(8,128)S(1)} all-reduce(f32[32,32]{0,1:T(8,128)S(1)} %convolution_bitcast_fusion.5), channel_id=1, replica_groups=mesh['rows'=8,'cols'=4] {'rows','cols'}, use_global_device_ids=true, to_apply=%region_10.11 | all-reduce | flops 1024 | bytes 8192 | tf_op jit(solution)/shard_map/psum | solution.py:98
  282.6 2.9 %cholesky.16 = f32[32,32]{1,0:T(8,128)S(1)} custom-call(f32[32,32]{1,0:T(8,128)S(1)} %fusion.31), custom_call_target="Cholesky" | custom-call | tf_op jit(solution)/shard_map/jit(cholesky)/cholesky | solution.py:101
  285.6 0.6 compare_reduce_fusion
  286.2 0.7 fusion.28
  286.9 2.4 custom-call.7
  289.3 1.1 fusion.29
  (45 shorter events, 1.0 us)
Async XLA Ops:
  0.0 7.3 %copy-start.1 = (f32[2048]{0:T(1024)S(1)}, f32[2048]{0:T(1024)}, u32[]{:S(2)}) copy-start(f32[2048]{0:T(1024)} %param.8) | copy-start | bytes 24580
  12.1 7.8 %collective-permute-start.2 = (f32[8,256]{1,0:T(8,128)S(1)}, f32[8,256]{1,0:T(8,128)S(1)}, u32[]{:S(2)}, u32[]{:S(2)}) collective-permute-start(f32[8,256]{1,0:T(8,128)S(1)} %get-tuple-element.17), channel_id=1, source_target_pairs={{0,1},{1,2},{2,3},{3,4},{4,5},{5,6},{6,7},{7,8},{8,9},{9,10},{10,1... | collective-permute-start | bytes 24584 | tf_op jit(solution)/shard_map/ppermute | solution.py:13
  12.6 7.4 %collective-permute-start.3 = (f32[8,256]{1,0:T(8,128)S(1)}, f32[8,256]{1,0:T(8,128)S(1)}, u32[]{:S(2)}, u32[]{:S(2)}) collective-permute-start(f32[8,256]{1,0:T(8,128)S(1)} %get-tuple-element.18), channel_id=1, source_target_pairs={{0,31},{1,0},{2,1},{3,2},{4,3},{5,4},{6,5},{7,6},{8,7},{9,8},{10,9... | collective-permute-start | bytes 24584 | tf_op jit(solution)/shard_map/ppermute | solution.py:13
  60.2 61.8 %copy-start = (bf16[32,2048]{1,0:T(8,128)(2,1)S(1)}, bf16[32,2048]{1,0:T(8,128)(2,1)}, u32[]{:S(2)}) copy-start(bf16[32,2048]{1,0:T(8,128)(2,1)} %param.9) | copy-start | bytes 393220
  65.0 6.7 %collective-permute-start.4 = (f32[8,256]{1,0:T(8,128)S(1)}, f32[8,256]{1,0:T(8,128)S(1)}, u32[]{:S(2)}, u32[]{:S(2)}) collective-permute-start(f32[8,256]{1,0:T(8,128)S(1)} %get-tuple-element.15), channel_id=1, source_target_pairs={{0,1},{1,2},{2,3},{3,4},{4,5},{5,6},{6,7},{7,8},{8,9},{9,10},{10,1... | collective-permute-start | bytes 24584 | tf_op jit(solution)/shard_map/ppermute | solution.py:13
  65.1 6.7 %collective-permute-start.5 = (f32[8,256]{1,0:T(8,128)S(1)}, f32[8,256]{1,0:T(8,128)S(1)}, u32[]{:S(2)}, u32[]{:S(2)}) collective-permute-start(f32[8,256]{1,0:T(8,128)S(1)} %get-tuple-element.16), channel_id=1, source_target_pairs={{0,31},{1,0},{2,1},{3,2},{4,3},{5,4},{6,5},{7,6},{8,7},{9,8},{10,9... | collective-permute-start | bytes 24584 | tf_op jit(solution)/shard_map/ppermute | solution.py:13
  116.7 6.7 %collective-permute-start.6 = (f32[8,256]{1,0:T(8,128)S(1)}, f32[8,256]{1,0:T(8,128)S(1)}, u32[]{:S(2)}, u32[]{:S(2)}) collective-permute-start(f32[8,256]{1,0:T(8,128)S(1)} %get-tuple-element.13), channel_id=1, source_target_pairs={{0,1},{1,2},{2,3},{3,4},{4,5},{5,6},{6,7},{7,8},{8,9},{9,10},{10,1... | collective-permute-start | bytes 24584 | tf_op jit(solution)/shard_map/ppermute | solution.py:13
  116.7 6.7 %collective-permute-start.7 = (f32[8,256]{1,0:T(8,128)S(1)}, f32[8,256]{1,0:T(8,128)S(1)}, u32[]{:S(2)}, u32[]{:S(2)}) collective-permute-start(f32[8,256]{1,0:T(8,128)S(1)} %get-tuple-element.14), channel_id=1, source_target_pairs={{0,31},{1,0},{2,1},{3,2},{4,3},{5,4},{6,5},{7,6},{8,7},{9,8},{10,9... | collective-permute-start | bytes 24584 | tf_op jit(solution)/shard_map/ppermute | solution.py:13
  122.1 111.9 %collective-permute-start.1 = (bf16[32,2048]{1,0:T(8,128)(2,1)S(1)}, bf16[32,2048]{1,0:T(8,128)(2,1)S(1)}, u32[]{:S(2)}, u32[]{:S(2)}) collective-permute-start(bf16[32,2048]{1,0:T(8,128)(2,1)S(1)} %copy-done), channel_id=1, source_target_pairs={{1,0},{2,1},{3,2},{4,3},{5,4},{6,5},{7,6},{8,7},{9,8},{10,9},{11,1... | collective-permute-start | bytes 393224 | tf_op jit(solution)/shard_map/ppermute | solution.py:25
  122.1 111.9 %collective-permute-start = (bf16[32,2048]{1,0:T(8,128)(2,1)S(1)}, bf16[32,2048]{1,0:T(8,128)(2,1)S(1)}, u32[]{:S(2)}, u32[]{:S(2)}) collective-permute-start(bf16[32,2048]{1,0:T(8,128)(2,1)S(1)} %copy-done), channel_id=1, source_target_pairs={{0,1},{1,2},{2,3},{3,4},{4,5},{5,6},{6,7},{7,8},{8,9},{9,10},{10,1... | collective-permute-start | bytes 393224 | tf_op jit(solution)/shard_map/ppermute | solution.py:22
  168.6 6.8 %collective-permute-start.8 = (f32[8,256]{1,0:T(8,128)S(1)}, f32[8,256]{1,0:T(8,128)S(1)}, u32[]{:S(2)}, u32[]{:S(2)}) collective-permute-start(f32[8,256]{1,0:T(8,128)S(1)} %get-tuple-element.11), channel_id=1, source_target_pairs={{0,1},{1,2},{2,3},{3,4},{4,5},{5,6},{6,7},{7,8},{8,9},{9,10},{10,1... | collective-permute-start | bytes 24584 | tf_op jit(solution)/shard_map/ppermute | solution.py:13
  168.6 6.7 %collective-permute-start.9 = (f32[8,256]{1,0:T(8,128)S(1)}, f32[8,256]{1,0:T(8,128)S(1)}, u32[]{:S(2)}, u32[]{:S(2)}) collective-permute-start(f32[8,256]{1,0:T(8,128)S(1)} %get-tuple-element.12), channel_id=1, source_target_pairs={{0,31},{1,0},{2,1},{3,2},{4,3},{5,4},{6,5},{7,6},{8,7},{9,8},{10,9... | collective-permute-start | bytes 24584 | tf_op jit(solution)/shard_map/ppermute | solution.py:13
  215.5 13.0 %collective-permute-start.10 = (f32[2048]{0:T(1024)S(1)}, f32[2048]{0:T(1024)S(1)}, u32[]{:S(2)}, u32[]{:S(2)}) collective-permute-start(f32[2048]{0:T(1024)S(1)} %bitcast.200), channel_id=1, source_target_pairs={{0,1},{1,2},{2,3},{3,4},{4,5},{5,6},{6,7},{7,8},{8,9},{9,10},{10,1... | collective-permute-start | bytes 24584 | tf_op jit(solution)/shard_map/ppermute | solution.py:22
  215.6 18.3 %collective-permute-start.11 = (f32[2048]{0:T(1024)S(1)}, f32[2048]{0:T(1024)S(1)}, u32[]{:S(2)}, u32[]{:S(2)}) collective-permute-start(f32[2048]{0:T(1024)S(1)} %bitcast.201), channel_id=1, source_target_pairs={{1,0},{2,1},{3,2},{4,3},{5,4},{6,5},{7,6},{8,7},{9,8},{10,9},{11,1... | collective-permute-start | bytes 24584 | tf_op jit(solution)/shard_map/ppermute | solution.py:25
  228.5 9.4 %collective-permute-start.12 = (f32[32,8,256]{2,0,1:T(8,128)S(1)}, f32[32,8,256]{2,0,1:T(8,128)S(1)}, u32[]{:S(2)}, u32[]{:S(2)}) collective-permute-start(f32[32,8,256]{2,0,1:T(8,128)S(1)} %get-tuple-element.9), channel_id=1, source_target_pairs={{0,1},{1,2},{2,3},{3,4},{4,5},{5,6},{6,7},{7,8},{8,9},{9,10},{10,1... | collective-permute-start | bytes 786440 | tf_op jit(solution)/shard_map/ppermute | solution.py:13
  228.6 9.4 %collective-permute-start.13 = (f32[32,8,256]{2,0,1:T(8,128)S(1)}, f32[32,8,256]{2,0,1:T(8,128)S(1)}, u32[]{:S(2)}, u32[]{:S(2)}) collective-permute-start(f32[32,8,256]{2,0,1:T(8,128)S(1)} %get-tuple-element.10), channel_id=1, source_target_pairs={{0,31},{1,0},{2,1},{3,2},{4,3},{5,4},{6,5},{7,6},{8,7},{9,8},{10,9... | collective-permute-start | bytes 786440 | tf_op jit(solution)/shard_map/ppermute | solution.py:13
where the time goes:
time: 292 us; the launch traced here: 290 us
  blocking collectives  194 us (66%)
  starting transfers between devices  33.9 us (12%)
  matrix products  33.6 us (12%)
  other arithmetic  16.4 us (6%)
  waiting for transfers between devices  8.2 us (3%)
  between operations  3.12 us (1%)
    psum x4, blocking collectives, per_device(): square_total = lax.psum(jnp.sum(raw_mass * raw_mass), ('rows', 'cols'))  156 us
    psum x1, blocking collectives, per_device(): lax.psum(jnp.dot(embedded, embedded.T, precision=lax.Precision.HIGHEST),...  38.3 us
    ppermute x10, starting transfers between devices, shifted(): lax.ppermute(shard, axis, [(i, (i + by) % devices) for i in range(devices)])  28 us
    dot_general x5, matrix products, spread_rows(): jnp.einsum('bkij,cbi->cbkj', tile_blocks, weighted, preferred_element_typ...  23.1 us
    ppermute x10, waiting for transfers between devices, shifted(): lax.ppermute(shard, axis, [(i, (i + by) % devices) for i in range(devices)])  8.19 us
    dot_general x1, matrix products, per_device(): jnp.einsum('bkij,cbkj->cbi', tile_blocks, gathered, preferred_element_typ...  5.94 us
  transfers between devices with their start and end apart: 14, of which 6 were waited for; matrix products, arithmetic and copies ran while one was open for 5% of the time, Pallas kernels for 0%

commit v1 on v0

v1 whole, which is shorter than its diff:
```python
import functools
import math

import jax
import jax.numpy as jnp
from jax import lax
from jax.experimental import pallas as pl
from jax.experimental.pallas import tpu as pltpu
from jax.sharding import PartitionSpec as P

POWER = 4
MESH = pl.DeviceIdType.MESH
F32 = jnp.float32
BF16 = jnp.bfloat16


def split3(value):
    high = value.astype(BF16)
    rest = value - high.astype(F32)
    middle = rest.astype(BF16)
    low = (rest - middle.astype(F32)).astype(BF16)
    return high, middle, low


def kernel(
    row_axis, col_axis, blocks, slots, tile, chans,
    cols_ref, count_ref, tiles_hbm, mass_ref, probe_ref, out_ref,
    tiles, place, window, landed, raw_halo, sums, probe_halo, scaled, products,
    low, mid, up, from_left, from_right, emb_parts, embedded, grams,
    load_sem, sum_send, sum_recv, win_send, win_recv, halo_send, halo_recv,
    probe_send, probe_recv, part_send, part_recv, gram_send, gram_recv,
):
    devices = row_axis * col_axis
    me = lax.axis_index("rows") * col_axis + lax.axis_index("cols")
    right = lax.rem(me + 1, devices)
    left = lax.rem(me + devices - 1, devices)
    total_blocks = devices * blocks
    pairs = blocks * slots
    span = 4 * blocks

    def place_of(device):
        return (device // col_axis, lax.rem(device, col_axis))

    def remote(src, dst, send, recv, device):
        return pltpu.make_async_remote_copy(
            src_ref=src, dst_ref=dst, send_sem=send, recv_sem=recv,
            device_id=place_of(device), device_id_type=MESH,
        )

    loads = [
        pltpu.make_async_copy(tiles_hbm.at[b], tiles.at[b], load_sem.at[b]) for b in range(blocks)
    ]
    for load in loads:
        load.start()

    barrier = pltpu.get_barrier_semaphore()

    def greet(step, carry):
        other = lax.rem(me + step, devices)
        pl.semaphore_signal(barrier, inc=1, device_id=place_of(other), device_id_type=MESH)
        return carry

    lax.fori_loop(1, devices, greet, 0)

    first = me * blocks
    spot = []
    alive = []
    for b in range(blocks):
        for k in range(slots):
            at = cols_ref[b, k] - first + blocks
            at = jnp.where(at < 0, at + total_blocks, at)
            at = jnp.where(at >= total_blocks, at - total_blocks, at)
            live = k < count_ref[b]
            spot.append(jnp.where(live, at, 3 * blocks))
            alive.append(live)
    rows_iota = lax.broadcasted_iota(jnp.int32, (span, 128), 0)
    lane3 = lax.rem(lax.broadcasted_iota(jnp.int32, (8, 3 * pairs), 1), pairs)
    spot_row = jnp.zeros((8, 3 * pairs), jnp.int32)
    for s in range(pairs):
        hit = jnp.where(rows_iota == spot[s], 1.0, 0.0)
        hit = jnp.where(rows_iota < 3 * blocks, hit, 0.0).astype(BF16)
        k = s % slots
        for part in range(tile // 128):
            place[s // slots, :, k * tile + part * 128 : k * tile + (part + 1) * 128] = hit
        spot_row = jnp.where(lane3 == s, spot[s], spot_row)
    rows3 = lax.broadcasted_iota(jnp.int32, (span, 3 * pairs), 0)
    place3 = jnp.where(rows3 == spot_row[0:1], 1.0, 0.0).astype(BF16)
    scaled[3 * blocks] = jnp.zeros((chans, tile), BF16)

    pl.semaphore_wait(barrier, devices - 1)

    probe_right = remote(probe_ref, probe_halo.at[0], probe_send.at[0], probe_recv.at[0], right)
    probe_left = remote(probe_ref, probe_halo.at[1], probe_send.at[1], probe_recv.at[1], left)
    probe_right.start()
    probe_left.start()

    contract_last = (((1,), (1,)), ((), ()))
    sum_rows = lax.broadcasted_iota(jnp.int32, (16, tile), 0)
    row_sum = jnp.zeros((16, tile), F32)
    for b in range(blocks):
        loads[b].wait()
        for k in range(slots):
            weight = jnp.where(alive[b * slots + k], 1.0, 0.0)
            chosen = jnp.where(sum_rows == b, weight, 0.0).astype(BF16)
            row_sum += lax.dot_general(
                chosen, tiles[b, k], contract_last, preferred_element_type=F32
            )
    row_inverse = 1.0 / row_sum[:blocks]

    def spread(step, stationary):
        weighted = (stationary * row_inverse).astype(BF16).astype(F32)
        total = jnp.zeros((span, tile), F32)
        for b in range(blocks):
            row = jnp.broadcast_to(weighted[b : b + 1], (span, tile)).astype(BF16)
            lhs = place[b] * jnp.concatenate([row] * slots, axis=1)
            total += jnp.dot(
                lhs, tiles[b].reshape(slots * tile, tile), preferred_element_type=F32
            )
        window[step] = total[: 3 * blocks]
        to_left = remote(
            window.at[step, pl.ds(0, blocks)], landed.at[step, 1],
            win_send.at[step, 0], win_recv.at[step, 1], left,
        )
        to_right = remote(
            window.at[step, pl.ds(2 * blocks, blocks)], landed.at[step, 0],
            win_send.at[step, 1], win_recv.at[step, 0], right,
        )
        to_left.start()
        to_right.start()
        to_left.wait_recv()
        to_right.wait_recv()
        arrived = total[blocks : 2 * blocks] + landed[step, 0] + landed[step, 1]
        return 0.85 * arrived + 0.15

    def push_all(buffer, send, recv):
        def push(offset, carry):
            other = lax.rem(me + offset, devices)
            remote(buffer.at[me], buffer.at[me], send, recv, other).start()
            return carry

        lax.fori_loop(1, devices, push, 0)

    def wait_all(buffer, sem):
        view = buffer.at[pl.ds(0, devices - 1)]
        pltpu.make_async_copy(view, view, sem).wait()

    def begin_norm(step, raw):
        square = raw * raw
        folded = square[:, :128]
        for part in range(1, tile // 128):
            folded += square[:, part * 128 : (part + 1) * 128]
        sums[step, me] = folded
        push_all(sums.at[step], sum_send.at[step], sum_recv.at[step])

    def end_norm(step):
        wait_all(sums.at[step], sum_recv.at[step])
        total = jnp.sum(sums[step], axis=0)
        total = jnp.sum(jnp.sum(total, axis=0, keepdims=True), axis=1, keepdims=True)
        return math.sqrt(total_blocks * tile) / jnp.sqrt(total)

    def power(step, stationary):
        raw = spread(step, stationary)
        begin_norm(step, raw)
        return raw * end_norm(step)

    stationary = lax.fori_loop(0, POWER - 1, power, mass_ref[...])
    raw = spread(POWER - 1, stationary)
    raw_halo[1] = raw
    raw_right = remote(raw_halo.at[1], raw_halo.at[0], halo_send.at[0], halo_recv.at[0], right)
    raw_left = remote(raw_halo.at[1], raw_halo.at[2], halo_send.at[1], halo_recv.at[1], left)
    raw_right.start()
    raw_left.start()
    begin_norm(POWER - 1, raw)
    norm = end_norm(POWER - 1)
    root = jnp.sqrt(raw * norm)
    root_inverse = 1.0 / root
    gain = root * row_inverse

    halves = tile // 128
    for b in range(blocks):
        probe = probe_ref[:, b * tile : (b + 1) * tile].astype(F32)
        pushed = (probe * gain[b : b + 1]).astype(BF16)
        for k in range(slots):
            product = jnp.dot(pushed, tiles[b, k], preferred_element_type=F32)
            at = (b * slots + k) * chans
            for h in range(halves):
                products[h, at : at + chans, :] = product[:, h * 128 : (h + 1) * 128]
    for c in range(chans):
        for h in range(halves):
            slab = products.at[h][pl.ds(c, pairs, stride=chans), :]
            parts = jnp.concatenate(split3(slab), axis=0)
            placed = jnp.dot(place3, parts, preferred_element_type=F32)
            low[h, c * blocks : (c + 1) * blocks, :] = placed[:blocks]
            mid[h, c * blocks : (c + 1) * blocks, :] = placed[blocks : 2 * blocks]
            up[h, c * blocks : (c + 1) * blocks, :] = placed[2 * blocks : 3 * blocks]
    part_left = remote(low, from_right, part_send.at[0], part_recv.at[0], left)
    part_right = remote(up, from_left, part_send.at[1], part_recv.at[1], right)
    part_left.start()
    part_right.start()

    probe_right.wait_recv()
    probe_left.wait_recv()
    raw_right.wait_recv()
    raw_left.wait_recv()
    for side, part in ((0, 0), (1, None), (2, 1)):
        if part is None:
            inverse = root_inverse
        else:
            inverse = 1.0 / jnp.sqrt(raw_halo[side] * norm)
        for b in range(blocks):
            lanes = slice(b * tile, (b + 1) * tile)
            probe = probe_ref[:, lanes] if part is None else probe_halo[part, :, lanes]
            scaled[side * blocks + b] = (probe.astype(F32) * inverse[b : b + 1]).astype(BF16)
    for b in range(blocks):
        forward = jnp.zeros((chans, tile), F32)
        for k in range(slots):
            forward += lax.dot_general(
                scaled[spot[b * slots + k]], tiles[b, k], contract_last,
                preferred_element_type=F32,
            )
        embedded[:, b * tile : (b + 1) * tile] = forward * gain[b : b + 1]

    part_left.wait_recv()
    part_right.wait_recv()
    for b in range(blocks):
        for h in range(halves):
            lanes = slice(b * tile + h * 128, b * tile + (h + 1) * 128)
            rows = pl.ds(b, chans, stride=blocks)
            arrived = mid.at[h][rows, :] + from_left.at[h][rows, :] + from_right.at[h][rows, :]
            back = arrived * root_inverse[b : b + 1, h * 128 : (h + 1) * 128]
            value = 0.5 * (embedded[:, lanes] + back)
            for index, piece in enumerate(split3(value)):
                emb_parts[index * chans : (index + 1) * chans, lanes] = piece

    cross = lax.dot_general(
        emb_parts[...], emb_parts[...], contract_last, preferred_element_type=F32
    )
    gram = jnp.zeros((chans, chans), F32)
    for i, j in ((2, 2), (1, 2), (2, 1), (0, 2), (2, 0), (1, 1), (0, 1), (1, 0), (0, 0)):
        gram += cross[i * chans : (i + 1) * chans, j * chans : (j + 1) * chans]
    groups = chans // 8
    grams[me] = jnp.concatenate([gram[g * 8 : (g + 1) * 8] for g in range(groups)], axis=1)
    push_all(grams, gram_send, gram_recv)
    wait_all(grams, gram_recv)
    packed = jnp.sum(grams[...], axis=0)
    gram = jnp.concatenate(
        [packed[:, g * chans : (g + 1) * chans] for g in range(groups)], axis=0
    )

    row_id = lax.broadcasted_iota(jnp.int32, (chans, chans), 0)
    col_id = lax.broadcasted_iota(jnp.int32, (chans, chans), 1)
    work = jnp.concatenate([gram, jnp.where(row_id == col_id, 1.0, 0.0)], axis=1)
    row_wide = lax.broadcasted_iota(jnp.int32, (chans, 2 * chans), 0)
    pivots = jnp.ones((chans, 2 * chans), F32)
    for k in range(chans):
        pivot = work[k : k + 1, k : k + 1]
        pivots = jnp.where(row_wide == k, pivot, pivots)
        scaled_row = work[k : k + 1] * (1.0 / pivot)
        below = jnp.where(row_wide > k, work[:, k : k + 1], 0.0)
        work = work - below * scaled_row
    inverse = (work * lax.rsqrt(pivots))[:, chans:]
    ih, im, il = split3(inverse)
    lhs = jnp.concatenate([ih, im, il, ih, im, ih], axis=1)
    eh = emb_parts[:chans]
    em = emb_parts[chans : 2 * chans]
    el = emb_parts[2 * chans :]
    rhs = jnp.concatenate([eh, eh, eh, em, em, el], axis=0)
    out_ref[...] = jnp.dot(lhs, rhs, preferred_element_type=F32)

    probe_right.wait_send()
    probe_left.wait_send()
    raw_right.wait_send()
    raw_left.wait_send()
    part_left.wait_send()
    part_right.wait_send()

    def drain(step, carry):
        wait_all(sums.at[step], sum_send.at[step])
        for side, at in ((0, 0), (1, 2 * blocks)):
            view = window.at[step, pl.ds(at, blocks)]
            pltpu.make_async_copy(view, view, win_send.at[step, side]).wait()
        return carry

    lax.fori_loop(0, POWER, drain, 0)
    wait_all(grams, gram_send)


def per_device(row_axis, col_axis, tile_blocks, tile_cols, tile_count, start_mass, probe_block):
    blocks, slots, tile = tile_blocks.shape[:3]
    chans = probe_block.shape[0]
    devices = row_axis * col_axis
    zones = blocks * tile
    halves = tile // 128
    vmem = pl.BlockSpec(memory_space=pltpu.VMEM)
    smem = pl.BlockSpec(memory_space=pltpu.SMEM)
    dma = pltpu.SemaphoreType.DMA
    part = pltpu.VMEM((halves, chans * blocks, 128), F32)
    return pl.pallas_call(
        functools.partial(kernel, row_axis, col_axis, blocks, slots, tile, chans),
        out_shape=jax.ShapeDtypeStruct((chans, zones), F32),
        in_specs=[smem, smem, pl.BlockSpec(memory_space=pl.ANY), vmem, vmem],
        out_specs=vmem,
        scratch_shapes=[
            pltpu.VMEM((blocks, slots, tile, tile), BF16),
            pltpu.VMEM((blocks, 4 * blocks, slots * tile), BF16),
            pltpu.VMEM((POWER, 3 * blocks, tile), F32),
            pltpu.VMEM((POWER, 2, blocks, tile), F32),
            pltpu.VMEM((3, blocks, tile), F32),
            pltpu.VMEM((POWER, devices, 8, 128), F32),
            pltpu.VMEM((2, chans, zones), BF16),
            pltpu.VMEM((3 * blocks + 1, chans, tile), BF16),
            pltpu.VMEM((halves, blocks * slots * chans, 128), F32),
            part, part, part, part, part,
            pltpu.VMEM((3 * chans, zones), BF16),
            pltpu.VMEM((chans, zones), F32),
            pltpu.VMEM((devices, 8, 128), F32),
            dma((blocks,)),
            dma((POWER,)), dma((POWER,)),
            dma((POWER, 2)), dma((POWER, 2)),
            dma((2,)), dma((2,)),
            dma((2,)), dma((2,)),
            dma((2,)), dma((2,)),
            dma, dma,
        ],
        compiler_params=pltpu.CompilerParams(
            collective_id=0, has_side_effects=True, vmem_limit_bytes=48 * 1024 * 1024
        ),
        name="embed",
    )(tile_cols, tile_count, tile_blocks, start_mass.reshape(blocks, tile), probe_block)


def solution(mesh):
    sizes = dict(mesh.shape)
    return jax.shard_map(
        functools.partial(per_device, sizes["rows"], sizes["cols"]),
        mesh=mesh,
        in_specs=(
            P(("rows", "cols"), None, None, None),
            P(("rows", "cols"), None),
            P(("rows", "cols")),
            P(("rows", "cols")),
            P(None, ("rows", "cols")),
        ),
        out_specs=P(None, ("rows", "cols")),
        check_vma=False,
    )
```

time: 292 us -> 79 us (0.27)
  blocking collectives: 194 us -> 0 us
  Pallas kernels: 0 us -> 75.1 us
  starting transfers between devices: 33.9 us -> 0 us
  matrix products: 33.6 us -> 0 us
  other arithmetic: 16.4 us -> 0 us
  waiting for transfers between devices: 8.2 us -> 0 us
  between operations: 3.12 us -> 0.01 us
    psum x5 -> x0, blocking collectives: 194 us -> none  [the longest x4 156 us: per_device(): square_total = lax.psum(jnp.sum(raw_mass * raw_mass), ('rows', 'cols'))]
    pallas_call x0 -> x1, Pallas kernels: none -> 75.1 us  [per_device(): pl.pallas_call(functools.partial(kernel, row_axis, col_axis, blocks, slot...]
    ppermute x14 -> x0, starting transfers between devices: 33.9 us -> none  [the longest x10 28 us: shifted(): lax.ppermute(shard, axis, [(i, (i + by) % devices) for i in range(devices)])]
    dot_general x12 -> x0, matrix products: 32.5 us -> none  [the longest x5 23.1 us: spread_rows(): jnp.einsum('bkij,cbi->cbkj', tile_blocks, weighted, preferred_element_typ...]
    ppermute x14 -> x0, waiting for transfers between devices: 8.2 us -> none  [the longest x10 8.19 us: shifted(): lax.ppermute(shard, axis, [(i, (i + by) % devices) for i in range(devices)])]
    reduce_sum x6 -> x0, other arithmetic: 8.12 us -> none  [the longest x1 5.61 us: per_device(): partial_rows = jnp.sum(tile_blocks, axis=3, dtype=jnp.float32)]
    another operation x5 -> x0, other arithmetic: 6.68 us -> none  [the longest x3 3.6 us: per_device(): lower_factor = jnp.linalg.cholesky(gram_matrix)]
  transfers between devices with their start and end apart: 14 -> 0, of which waited for: 6 -> 0; matrix products, arithmetic and copies ran while one was open for 5% -> 0% of each run, Pallas kernels for 0% -> 0%
where the time goes in v1:
time: 79 us; the launch traced here: 78.8 us
  Pallas kernels  75.1 us (95%)
  local copies, waits for them, and re-layouts  3.65 us (5%)
    pallas_call x1, Pallas kernels, per_device(): pl.pallas_call(functools.partial(kernel, row_axis, col_axis, blocks, slot...  75.1 us
    unnamed x7, local copies, waits for them, and re-layouts  2.95 us

profile of v1, /device:TPU:0, one launch (start us, length us, event | category | flops | bytes accessed | tf_op | source)
XLA Modules:
  0.0 78.8 jit_solution(7718432681521000609)
XLA Ops:
  0.0 0.7 reshape.3.mass_ref
  0.7 0.0 copy-start
  0.7 0.9 %copy-done = bf16[32,2048]{1,0:T(8,128)(2,1)S(1)} copy-done((bf16[32,2048]{1,0:T(8,128)(2,1)S(1)}, bf16[32,2048]{1,0:T(8,128)(2,1)}, u32[]{:S(2)}) %copy-start) | copy-done | bytes 131096
  1.6 0.0 copy-start.1
  1.6 0.7 copy-done.1
  2.3 0.0 copy-start.2
  2.3 0.7 copy-done.2
  2.9 75.1 %embed.1 = f32[32,2048]{1,0:T(8,128)S(1)} custom-call(s32[8,8]{1,0:T(8,128)S(1)} %copy-done.1, s32[8]{0:T(128)S(1)} %copy-done.2, bf16[8,8,256,256]{3,2,1,0:T(8,128)(2,1)} %tiles_hbm.1, f32[8,256]{1,0:T(8,128)S(1)} %reshape.3.mass_ref, bf16[32,2048]{1,0:T(8,128)(2,1)S(1)} %copy-done), custom_call_target="tpu_custom_call" | custom-call | tf_op jit(solution)/shard_map/embed/pallas_call | solution.py:298
  78.1 0.7 copy.7
Async XLA Ops:
  0.7 0.9 %copy-start = (bf16[32,2048]{1,0:T(8,128)(2,1)S(1)}, bf16[32,2048]{1,0:T(8,128)(2,1)}, u32[]{:S(2)}) copy-start(bf16[32,2048]{1,0:T(8,128)(2,1)} %probe_ref.1) | copy-start | bytes 393220
  1.6 0.7 copy-start.1
  2.3 0.7 copy-start.2

commit v2 on v1

--- a/solution.py
+++ b/solution.py
@@ -23,11 +23,13 @@
 
 
 def kernel(
-    row_axis, col_axis, blocks, slots, tile, chans,
-    cols_ref, count_ref, tiles_hbm, mass_ref, probe_ref, out_ref,
-    tiles, place, window, landed, raw_halo, sums, probe_halo, scaled, products,
-    low, mid, up, from_left, from_right, emb_parts, embedded, grams,
-    load_sem, sum_send, sum_recv, win_send, win_recv, halo_send, halo_recv,
+    row_axis, col_axis, group, blocks, slots, tile, chans,
+    cols_hbm, count_hbm, tiles_hbm, mass_hbm, probe_hbm, out_ref,
+    cols_ref, count_ref, mass_ref, probe_ref,
+    tiles, place, window, landed, raw_halo, near_sums, far_sums, probe_halo, scaled, products,
+    low, mid, up, from_left, from_right, emb_parts, embedded, near_grams, far_grams,
+    small_sem, load_sem, near_send, near_recv, far_send, far_recv,
+    win_send, win_recv, halo_send, halo_recv,
     probe_send, probe_recv, part_send, part_recv, gram_send, gram_recv,
 ):
     devices = row_axis * col_axis
@@ -37,6 +39,9 @@
     total_blocks = devices * blocks
     pairs = blocks * slots
     span = 4 * blocks
+    groups = devices // group
+    my_group = me // group
+    my_member = lax.rem(me, group)
 
     def place_of(device):
         return (device // col_axis, lax.rem(device, col_axis))
@@ -47,6 +52,14 @@
             device_id=place_of(device), device_id_type=MESH,
         )
 
+    smalls = [
+        pltpu.make_async_copy(src, dst, small_sem.at[i])
+        for i, (src, dst) in enumerate(
+            ((cols_hbm, cols_ref), (count_hbm, count_ref), (probe_hbm, probe_ref), (mass_hbm, mass_ref))
+        )
+    ]
+    for small in smalls:
+        small.start()
     loads = [
         pltpu.make_async_copy(tiles_hbm.at[b], tiles.at[b], load_sem.at[b]) for b in range(blocks)
     ]
@@ -55,12 +68,28 @@
 
     barrier = pltpu.get_barrier_semaphore()
 
-    def greet(step, carry):
-        other = lax.rem(me + step, devices)
+    def near(offset):
+        return my_group * group + lax.rem(my_member + offset, group)
+
+    def far(offset):
+        return lax.rem(my_group + offset, groups) * group + my_member
+
+    def greet(other):
         pl.semaphore_signal(barrier, inc=1, device_id=place_of(other), device_id_type=MESH)
-        return carry
-
-    lax.fori_loop(1, devices, greet, 0)
+
+    def each(count, action):
+        def body(offset, carry):
+            action(offset)
+            return carry
+
+        lax.fori_loop(1, count, body, 0, unroll=count <= 8)
+
+    greet(left)
+    greet(right)
+    each(group, lambda offset: greet(near(offset)))
+    each(groups, lambda offset: greet(far(offset)))
+    smalls[0].wait()
+    smalls[1].wait()
 
     first = me * blocks
     spot = []
@@ -87,7 +116,8 @@
     place3 = jnp.where(rows3 == spot_row[0:1], 1.0, 0.0).astype(BF16)
     scaled[3 * blocks] = jnp.zeros((chans, tile), BF16)
 
-    pl.semaphore_wait(barrier, devices - 1)
+    smalls[2].wait()
+    pl.semaphore_wait(barrier, group + groups)
 
     probe_right = remote(probe_ref, probe_halo.at[0], probe_send.at[0], probe_recv.at[0], right)
     probe_left = remote(probe_ref, probe_halo.at[1], probe_send.at[1], probe_recv.at[1], left)
@@ -107,8 +137,46 @@
             )
     row_inverse = 1.0 / row_sum[:blocks]
 
-    def spread(step, stationary):
-        weighted = (stationary * row_inverse).astype(BF16).astype(F32)
+    def push_near(buffer, send, recv):
+        each(
+            group,
+            lambda offset: remote(
+                buffer.at[my_member], buffer.at[my_member], send, recv, near(offset)
+            ).start(),
+        )
+
+    def push_far(buffer, send, recv):
+        each(
+            groups,
+            lambda offset: remote(
+                buffer.at[my_group], buffer.at[my_group], send, recv, far(offset)
+            ).start(),
+        )
+
+    def wait_all(buffer, sem, count):
+        view = buffer.at[pl.ds(0, count - 1)]
+        pltpu.make_async_copy(view, view, sem).wait()
+
+    def norm_near(step, raw):
+        square = raw * raw
+        folded = square[:, :128]
+        for part in range(1, tile // 128):
+            folded += square[:, part * 128 : (part + 1) * 128]
+        near_sums[step, my_member] = jnp.sum(folded, axis=0, keepdims=True)
+        push_near(near_sums.at[step], near_send.at[step], near_recv.at[step])
+
+    def norm_far(step):
+        wait_all(near_sums.at[step], near_recv.at[step], group)
+        far_sums[step, my_group] = jnp.sum(near_sums[step], axis=0)
+        push_far(far_sums.at[step], far_send.at[step], far_recv.at[step])
+
+    def norm_end(step):
+        wait_all(far_sums.at[step], far_recv.at[step], groups)
+        total = jnp.sum(jnp.sum(far_sums[step], axis=0), axis=1, keepdims=True)
+        return math.sqrt(total_blocks * tile) / jnp.sqrt(total)
+
+    def spread(step, mass):
+        weighted = (mass * row_inverse).astype(BF16).astype(F32)
         total = jnp.zeros((span, tile), F32)
         for b in range(blocks):
             row = jnp.broadcast_to(weighted[b : b + 1], (span, tile)).astype(BF16)
@@ -132,46 +200,26 @@
         arrived = total[blocks : 2 * blocks] + landed[step, 0] + landed[step, 1]
         return 0.85 * arrived + 0.15
 
-    def push_all(buffer, send, recv):
-        def push(offset, carry):
-            other = lax.rem(me + offset, devices)
-            remote(buffer.at[me], buffer.at[me], send, recv, other).start()
-            return carry
-
-        lax.fori_loop(1, devices, push, 0)
-
-    def wait_all(buffer, sem):
-        view = buffer.at[pl.ds(0, devices - 1)]
-        pltpu.make_async_copy(view, view, sem).wait()
-
-    def begin_norm(step, raw):
-        square = raw * raw
-        folded = square[:, :128]
-        for part in range(1, tile // 128):
-            folded += square[:, part * 128 : (part + 1) * 128]
-        sums[step, me] = folded
-        push_all(sums.at[step], sum_send.at[step], sum_recv.at[step])
-
-    def end_norm(step):
-        wait_all(sums.at[step], sum_recv.at[step])
-        total = jnp.sum(sums[step], axis=0)
-        total = jnp.sum(jnp.sum(total, axis=0, keepdims=True), axis=1, keepdims=True)
-        return math.sqrt(total_blocks * tile) / jnp.sqrt(total)
-
-    def power(step, stationary):
-        raw = spread(step, stationary)
-        begin_norm(step, raw)
-        return raw * end_norm(step)
-
-    stationary = lax.fori_loop(0, POWER - 1, power, mass_ref[...])
-    raw = spread(POWER - 1, stationary)
+    smalls[3].wait()
+    start = jnp.concatenate(
+        [mass_ref[pl.ds(b * tile, tile)].reshape(1, tile) for b in range(blocks)], axis=0
+    )
+
+    def power(step, mass):
+        raw = spread(step, mass)
+        norm_near(step, raw)
+        norm_far(step)
+        return raw * norm_end(step)
+
+    raw = spread(POWER - 1, lax.fori_loop(0, POWER - 1, power, start))
+    norm_near(POWER - 1, raw)
     raw_halo[1] = raw
     raw_right = remote(raw_halo.at[1], raw_halo.at[0], halo_send.at[0], halo_recv.at[0], right)
     raw_left = remote(raw_halo.at[1], raw_halo.at[2], halo_send.at[1], halo_recv.at[1], left)
     raw_right.start()
     raw_left.start()
-    begin_norm(POWER - 1, raw)
-    norm = end_norm(POWER - 1)
+    norm_far(POWER - 1)
+    norm = norm_end(POWER - 1)
     root = jnp.sqrt(raw * norm)
     root_inverse = 1.0 / root
     gain = root * row_inverse
@@ -185,18 +233,20 @@
             at = (b * slots + k) * chans
             for h in range(halves):
                 products[h, at : at + chans, :] = product[:, h * 128 : (h + 1) * 128]
-    for c in range(chans):
-        for h in range(halves):
+    part_copies = []
+    for h in range(halves):
+        for c in range(chans):
             slab = products.at[h][pl.ds(c, pairs, stride=chans), :]
             parts = jnp.concatenate(split3(slab), axis=0)
             placed = jnp.dot(place3, parts, preferred_element_type=F32)
             low[h, c * blocks : (c + 1) * blocks, :] = placed[:blocks]
             mid[h, c * blocks : (c + 1) * blocks, :] = placed[blocks : 2 * blocks]
             up[h, c * blocks : (c + 1) * blocks, :] = placed[2 * blocks : 3 * blocks]
-    part_left = remote(low, from_right, part_send.at[0], part_recv.at[0], left)
-    part_right = remote(up, from_left, part_send.at[1], part_recv.at[1], right)
-    part_left.start()
-    part_right.start()
+        to_left = remote(low.at[h], from_right.at[h], part_send.at[0, h], part_recv.at[0, h], left)
+        to_right = remote(up.at[h], from_left.at[h], part_send.at[1, h], part_recv.at[1, h], right)
+        to_left.start()
+        to_right.start()
+        part_copies += [to_left, to_right]
 
     probe_right.wait_recv()
     probe_left.wait_recv()
@@ -220,8 +270,8 @@
             )
         embedded[:, b * tile : (b + 1) * tile] = forward * gain[b : b + 1]
 
-    part_left.wait_recv()
-    part_right.wait_recv()
+    for copy in part_copies:
+        copy.wait_recv()
     for b in range(blocks):
         for h in range(halves):
             lanes = slice(b * tile + h * 128, b * tile + (h + 1) * 128)
@@ -238,26 +288,48 @@
     gram = jnp.zeros((chans, chans), F32)
     for i, j in ((2, 2), (1, 2), (2, 1), (0, 2), (2, 0), (1, 1), (0, 1), (1, 0), (0, 0)):
         gram += cross[i * chans : (i + 1) * chans, j * chans : (j + 1) * chans]
-    groups = chans // 8
-    grams[me] = jnp.concatenate([gram[g * 8 : (g + 1) * 8] for g in range(groups)], axis=1)
-    push_all(grams, gram_send, gram_recv)
-    wait_all(grams, gram_recv)
-    packed = jnp.sum(grams[...], axis=0)
+    quarters = chans // 8
+    near_grams[my_member] = jnp.concatenate(
+        [gram[q * 8 : (q + 1) * 8] for q in range(quarters)], axis=1
+    )
+    push_near(near_grams, gram_send.at[0], gram_recv.at[0])
+    wait_all(near_grams, gram_recv.at[0], group)
+    far_grams[my_group] = jnp.sum(near_grams[...], axis=0)
+    push_far(far_grams, gram_send.at[1], gram_recv.at[1])
+    wait_all(far_grams, gram_recv.at[1], groups)
+    packed = jnp.sum(far_grams[...], axis=0)
     gram = jnp.concatenate(
-        [packed[:, g * chans : (g + 1) * chans] for g in range(groups)], axis=0
+        [packed[:, q * chans : (q + 1) * chans] for q in range(quarters)], axis=0
     )
 
+    wide = (chans, 2 * chans)
     row_id = lax.broadcasted_iota(jnp.int32, (chans, chans), 0)
     col_id = lax.broadcasted_iota(jnp.int32, (chans, chans), 1)
     work = jnp.concatenate([gram, jnp.where(row_id == col_id, 1.0, 0.0)], axis=1)
-    row_wide = lax.broadcasted_iota(jnp.int32, (chans, 2 * chans), 0)
-    pivots = jnp.ones((chans, 2 * chans), F32)
-    for k in range(chans):
-        pivot = work[k : k + 1, k : k + 1]
-        pivots = jnp.where(row_wide == k, pivot, pivots)
-        scaled_row = work[k : k + 1] * (1.0 / pivot)
-        below = jnp.where(row_wide > k, work[:, k : k + 1], 0.0)
-        work = work - below * scaled_row
+    row_wide = lax.broadcasted_iota(jnp.int32, wide, 0)
+    pivots = jnp.ones(wide, F32)
+    panel = 4
+    for k in range(0, chans, panel):
+        rows = [jnp.broadcast_to(work[k + i : k + i + 1], wide) for i in range(panel)]
+        columns = [
+            jnp.broadcast_to(work[:, k + i : k + i + 1], wide) for i in range(panel)
+        ]
+        corner = [
+            [jnp.broadcast_to(columns[j][k + i : k + i + 1], wide) for j in range(i + 1)]
+            for i in range(panel)
+        ]
+        for j in range(panel):
+            pivots = jnp.where(row_wide == k + j, corner[j][j], pivots)
+            inverse_pivot = 1.0 / corner[j][j]
+            factors = [corner[i][j] * inverse_pivot for i in range(j + 1, panel)]
+            for i in range(j + 1, panel):
+                factor = factors[i - j - 1]
+                rows[i] = rows[i] - factor * rows[j]
+                columns[i] = columns[i] - factor * columns[j]
+                for m in range(j + 1, i + 1):
+                    corner[i][m] = corner[i][m] - factor * corner[m][j]
+            below = jnp.where(row_wide > k + j, columns[j], 0.0)
+            work = work - below * (rows[j] * inverse_pivot)
     inverse = (work * lax.rsqrt(pivots))[:, chans:]
     ih, im, il = split3(inverse)
     lhs = jnp.concatenate([ih, im, il, ih, im, ih], axis=1)
@@ -271,18 +343,20 @@
     probe_left.wait_send()
     raw_right.wait_send()
     raw_left.wait_send()
-    part_left.wait_send()
-    part_right.wait_send()
+    for copy in part_copies:
+        copy.wait_send()
 
     def drain(step, carry):
-        wait_all(sums.at[step], sum_send.at[step])
+        wait_all(near_sums.at[step], near_send.at[step], group)
+        wait_all(far_sums.at[step], far_send.at[step], groups)
         for side, at in ((0, 0), (1, 2 * blocks)):
             view = window.at[step, pl.ds(at, blocks)]
             pltpu.make_async_copy(view, view, win_send.at[step, side]).wait()
         return carry
 
     lax.fori_loop(0, POWER, drain, 0)
-    wait_all(grams, gram_send)
+    wait_all(near_grams, gram_send.at[0], group)
+    wait_all(far_grams, gram_send.at[1], groups)
 
 
 def per_device(row_axis, col_axis, tile_blocks, tile_cols, tile_count, start_mass, probe_block):
@@ -292,41 +366,51 @@
     zones = blocks * tile
     halves = tile // 128
     vmem = pl.BlockSpec(memory_space=pltpu.VMEM)
-    smem = pl.BlockSpec(memory_space=pltpu.SMEM)
+    in_hbm = pl.BlockSpec(memory_space=pltpu.HBM)
+    group = min(8, devices)
+    groups = devices // group
     dma = pltpu.SemaphoreType.DMA
     part = pltpu.VMEM((halves, chans * blocks, 128), F32)
     return pl.pallas_call(
-        functools.partial(kernel, row_axis, col_axis, blocks, slots, tile, chans),
+        functools.partial(kernel, row_axis, col_axis, group, blocks, slots, tile, chans),
         out_shape=jax.ShapeDtypeStruct((chans, zones), F32),
-        in_specs=[smem, smem, pl.BlockSpec(memory_space=pl.ANY), vmem, vmem],
+        in_specs=[in_hbm] * 5,
         out_specs=vmem,
         scratch_shapes=[
+            pltpu.SMEM(tile_cols.shape, jnp.int32),
+            pltpu.SMEM(tile_count.shape, jnp.int32),
+            pltpu.VMEM(start_mass.shape, F32),
+            pltpu.VMEM(probe_block.shape, BF16),
             pltpu.VMEM((blocks, slots, tile, tile), BF16),
             pltpu.VMEM((blocks, 4 * blocks, slots * tile), BF16),
             pltpu.VMEM((POWER, 3 * blocks, tile), F32),
             pltpu.VMEM((POWER, 2, blocks, tile), F32),
             pltpu.VMEM((3, blocks, tile), F32),
-            pltpu.VMEM((POWER, devices, 8, 128), F32),
+            pltpu.VMEM((POWER, group, 1, 128), F32),
+            pltpu.VMEM((POWER, groups, 1, 128), F32),
             pltpu.VMEM((2, chans, zones), BF16),
             pltpu.VMEM((3 * blocks + 1, chans, tile), BF16),
             pltpu.VMEM((halves, blocks * slots * chans, 128), F32),
             part, part, part, part, part,
             pltpu.VMEM((3 * chans, zones), BF16),
             pltpu.VMEM((chans, zones), F32),
-            pltpu.VMEM((devices, 8, 128), F32),
+            pltpu.VMEM((group, 8, 128), F32),
+            pltpu.VMEM((groups, 8, 128), F32),
+            dma((4,)),
             dma((blocks,)),
+            dma((POWER,)), dma((POWER,)),
             dma((POWER,)), dma((POWER,)),
             dma((POWER, 2)), dma((POWER, 2)),
             dma((2,)), dma((2,)),
             dma((2,)), dma((2,)),
+            dma((2, halves)), dma((2, halves)),
             dma((2,)), dma((2,)),
-            dma, dma,
         ],
         compiler_params=pltpu.CompilerParams(
-            collective_id=0, has_side_effects=True, vmem_limit_bytes=48 * 1024 * 1024
+            collective_id=0, has_side_effects=True, vmem_limit_bytes=64 * 1024 * 1024
         ),
         name="embed",
-    )(tile_cols, tile_count, tile_blocks, start_mass.reshape(blocks, tile), probe_block)
+    )(tile_cols, tile_count, tile_blocks, start_mass, probe_block)
 
 
 def solution(mesh):

time: 79 us -> 79.7 us (level)
  Pallas kernels: 75.1 us -> 77.9 us
  local copies, waits for them, and re-layouts: 3.65 us -> 1.67 us
    pallas_call x1, Pallas kernels: 75.1 us -> 77.9 us  [per_device(): pl.pallas_call(functools.partial(kernel, row_axis, col_axis, group, block...]
    unnamed x7 -> x1, local copies, waits for them, and re-layouts: 2.95 us -> 1.67 us
where the time goes in v2:
time: 79.7 us; the launch traced here: 79.6 us
  Pallas kernels  77.9 us (98%)
  local copies, waits for them, and re-layouts  1.67 us (2%)
    pallas_call x1, Pallas kernels, per_device(): pl.pallas_call(functools.partial(kernel, row_axis, col_axis, group, block...  77.9 us
    unnamed x1, local copies, waits for them, and re-layouts  1.67 us

profile of v2, /device:TPU:0, one launch (start us, length us, event | category | flops | bytes accessed | tf_op | source)
XLA Modules:
  0.0 79.6 jit_solution(9800417531234807021)
XLA Ops:
  0.0 77.9 %embed.1 = f32[32,2048]{1,0:T(8,128)} custom-call(s32[8,8]{1,0:T(8,128)} %cols_hbm.1, s32[8]{0:T(128)} %count_hbm.1, bf16[8,8,256,256]{3,2,1,0:T(8,128)(2,1)} %tiles_hbm.1, f32[2048]{0:T(1024)} %mass_hbm.1, bf16[32,2048]{1,0:T(8,128)(2,1)} %probe_hbm.1), custom_call_target="tpu_custom_call" | custom-call | tf_op jit(solution)/shard_map/embed/pallas_call | solution.py:374
  77.9 1.7 %copy.7 = f32[32,2048]{1,0:T(8,128)} copy(f32[32,2048]{1,0:T(8,128)} %embed.1) | data formatting | bytes 524288

commit v3 on v2

--- a/solution.py
+++ b/solution.py
@@ -26,9 +26,9 @@
     row_axis, col_axis, group, blocks, slots, tile, chans,
     cols_hbm, count_hbm, tiles_hbm, mass_hbm, probe_hbm, out_ref,
     cols_ref, count_ref, mass_ref, probe_ref,
-    tiles, place, window, landed, raw_halo, near_sums, far_sums, probe_halo, scaled, products,
+    tiles, place, window, landed, raw_halo, sums, probe_halo, scaled, products,
     low, mid, up, from_left, from_right, emb_parts, embedded, near_grams, far_grams,
-    small_sem, load_sem, near_send, near_recv, far_send, far_recv,
+    small_sem, load_sem, sum_send, sum_recv,
     win_send, win_recv, halo_send, halo_recv,
     probe_send, probe_recv, part_send, part_recv, gram_send, gram_recv,
 ):
@@ -82,12 +82,9 @@
             action(offset)
             return carry
 
-        lax.fori_loop(1, count, body, 0, unroll=count <= 8)
-
-    greet(left)
-    greet(right)
-    each(group, lambda offset: greet(near(offset)))
-    each(groups, lambda offset: greet(far(offset)))
+        lax.fori_loop(1, count, body, 0, unroll=count <= 32)
+
+    each(devices, lambda offset: greet(lax.rem(me + offset, devices)))
     smalls[0].wait()
     smalls[1].wait()
 
@@ -117,7 +114,7 @@
     scaled[3 * blocks] = jnp.zeros((chans, tile), BF16)
 
     smalls[2].wait()
-    pl.semaphore_wait(barrier, group + groups)
+    pl.semaphore_wait(barrier, devices - 1)
 
     probe_right = remote(probe_ref, probe_halo.at[0], probe_send.at[0], probe_recv.at[0], right)
     probe_left = remote(probe_ref, probe_halo.at[1], probe_send.at[1], probe_recv.at[1], left)
@@ -157,22 +154,26 @@
         view = buffer.at[pl.ds(0, count - 1)]
         pltpu.make_async_copy(view, view, sem).wait()
 
-    def norm_near(step, raw):
+    def other(offset):
+        return lax.rem(me + offset, devices)
+
+    def norm_begin(step, raw):
         square = raw * raw
         folded = square[:, :128]
         for part in range(1, tile // 128):
             folded += square[:, part * 128 : (part + 1) * 128]
-        near_sums[step, my_member] = jnp.sum(folded, axis=0, keepdims=True)
-        push_near(near_sums.at[step], near_send.at[step], near_recv.at[step])
-
-    def norm_far(step):
-        wait_all(near_sums.at[step], near_recv.at[step], group)
-        far_sums[step, my_group] = jnp.sum(near_sums[step], axis=0)
-        push_far(far_sums.at[step], far_send.at[step], far_recv.at[step])
+        sums[step, me] = jnp.sum(folded, axis=0, keepdims=True)
+        each(
+            devices,
+            lambda offset: remote(
+                sums.at[step, me], sums.at[step, me], sum_send.at[step], sum_recv.at[step],
+                other(offset),
+            ).start(),
+        )
 
     def norm_end(step):
-        wait_all(far_sums.at[step], far_recv.at[step], groups)
-        total = jnp.sum(jnp.sum(far_sums[step], axis=0), axis=1, keepdims=True)
+        wait_all(sums.at[step], sum_recv.at[step], devices)
+        total = jnp.sum(jnp.sum(sums[step], axis=0), axis=1, keepdims=True)
         return math.sqrt(total_blocks * tile) / jnp.sqrt(total)
 
     def spread(step, mass):
@@ -207,18 +208,16 @@
 
     def power(step, mass):
         raw = spread(step, mass)
-        norm_near(step, raw)
-        norm_far(step)
+        norm_begin(step, raw)
         return raw * norm_end(step)
 
     raw = spread(POWER - 1, lax.fori_loop(0, POWER - 1, power, start))
-    norm_near(POWER - 1, raw)
+    norm_begin(POWER - 1, raw)
     raw_halo[1] = raw
     raw_right = remote(raw_halo.at[1], raw_halo.at[0], halo_send.at[0], halo_recv.at[0], right)
     raw_left = remote(raw_halo.at[1], raw_halo.at[2], halo_send.at[1], halo_recv.at[1], left)
     raw_right.start()
     raw_left.start()
-    norm_far(POWER - 1)
     norm = norm_end(POWER - 1)
     root = jnp.sqrt(raw * norm)
     root_inverse = 1.0 / root
@@ -234,16 +233,28 @@
             for h in range(halves):
                 products[h, at : at + chans, :] = product[:, h * 128 : (h + 1) * 128]
     part_copies = []
-    for h in range(halves):
-        for c in range(chans):
-            slab = products.at[h][pl.ds(c, pairs, stride=chans), :]
+    for chunk in range(2):
+        begin, end = chunk * chans // 2, (chunk + 1) * chans // 2
+        for c in range(begin, end):
+            slab = jnp.concatenate(
+                [products.at[h][pl.ds(c, pairs, stride=chans), :] for h in range(halves)], axis=1
+            )
             parts = jnp.concatenate(split3(slab), axis=0)
             placed = jnp.dot(place3, parts, preferred_element_type=F32)
-            low[h, c * blocks : (c + 1) * blocks, :] = placed[:blocks]
-            mid[h, c * blocks : (c + 1) * blocks, :] = placed[blocks : 2 * blocks]
-            up[h, c * blocks : (c + 1) * blocks, :] = placed[2 * blocks : 3 * blocks]
-        to_left = remote(low.at[h], from_right.at[h], part_send.at[0, h], part_recv.at[0, h], left)
-        to_right = remote(up.at[h], from_left.at[h], part_send.at[1, h], part_recv.at[1, h], right)
+            for h in range(halves):
+                column = placed[:, h * 128 : (h + 1) * 128]
+                low[h, c * blocks : (c + 1) * blocks, :] = column[:blocks]
+                mid[h, c * blocks : (c + 1) * blocks, :] = column[blocks : 2 * blocks]
+                up[h, c * blocks : (c + 1) * blocks, :] = column[2 * blocks : 3 * blocks]
+        some = pl.ds(begin * blocks, (end - begin) * blocks)
+        to_left = remote(
+            low.at[:, some], from_right.at[:, some],
+            part_send.at[0, chunk], part_recv.at[0, chunk], left,
+        )
+        to_right = remote(
+            up.at[:, some], from_left.at[:, some],
+            part_send.at[1, chunk], part_recv.at[1, chunk], right,
+        )
         to_left.start()
         to_right.start()
         part_copies += [to_left, to_right]
@@ -347,8 +358,7 @@
         copy.wait_send()
 
     def drain(step, carry):
-        wait_all(near_sums.at[step], near_send.at[step], group)
-        wait_all(far_sums.at[step], far_send.at[step], groups)
+        wait_all(sums.at[step], sum_send.at[step], devices)
         for side, at in ((0, 0), (1, 2 * blocks)):
             view = window.at[step, pl.ds(at, blocks)]
             pltpu.make_async_copy(view, view, win_send.at[step, side]).wait()
@@ -386,8 +396,7 @@
             pltpu.VMEM((POWER, 3 * blocks, tile), F32),
             pltpu.VMEM((POWER, 2, blocks, tile), F32),
             pltpu.VMEM((3, blocks, tile), F32),
-            pltpu.VMEM((POWER, group, 1, 128), F32),
-            pltpu.VMEM((POWER, groups, 1, 128), F32),
+            pltpu.VMEM((POWER, devices, 1, 128), F32),
             pltpu.VMEM((2, chans, zones), BF16),
             pltpu.VMEM((3 * blocks + 1, chans, tile), BF16),
             pltpu.VMEM((halves, blocks * slots * chans, 128), F32),
@@ -399,11 +408,10 @@
             dma((4,)),
             dma((blocks,)),
             dma((POWER,)), dma((POWER,)),
-            dma((POWER,)), dma((POWER,)),
             dma((POWER, 2)), dma((POWER, 2)),
             dma((2,)), dma((2,)),
             dma((2,)), dma((2,)),
-            dma((2, halves)), dma((2, halves)),
+            dma((2, 2)), dma((2, 2)),
             dma((2,)), dma((2,)),
         ],
         compiler_params=pltpu.CompilerParams(

time: 79.7 us -> 72 us (0.903)
  Pallas kernels: 77.9 us -> 70.2 us
    pallas_call x1, Pallas kernels: 77.9 us -> 70.2 us  [per_device(): pl.pallas_call(functools.partial(kernel, row_axis, col_axis, group, block...]
where the time goes in v3:
time: 72 us; the launch traced here: 71.9 us
  Pallas kernels  70.2 us (98%)
  local copies, waits for them, and re-layouts  1.67 us (2%)
    pallas_call x1, Pallas kernels, per_device(): pl.pallas_call(functools.partial(kernel, row_axis, col_axis, group, block...  70.2 us
    unnamed x1, local copies, waits for them, and re-layouts  1.67 us

profile of v3, /device:TPU:0, one launch (start us, length us, event | category | flops | bytes accessed | tf_op | source)
XLA Modules:
  0.0 71.9 jit_solution(9110327789475994322)
XLA Ops:
  0.0 70.2 %embed.1 = f32[32,2048]{1,0:T(8,128)} custom-call(s32[8,8]{1,0:T(8,128)} %cols_hbm.1, s32[8]{0:T(128)} %count_hbm.1, bf16[8,8,256,256]{3,2,1,0:T(8,128)(2,1)} %tiles_hbm.1, f32[2048]{0:T(1024)} %mass_hbm.1, bf16[32,2048]{1,0:T(8,128)(2,1)} %probe_hbm.1), custom_call_target="tpu_custom_call" | custom-call | tf_op jit(solution)/shard_map/embed/pallas_call | solution.py:384
  70.2 1.7 %copy.7 = f32[32,2048]{1,0:T(8,128)} copy(f32[32,2048]{1,0:T(8,128)} %embed.1) | data formatting | bytes 524288

commit v4 on v3

--- a/solution.py
+++ b/solution.py
@@ -111,7 +111,7 @@
         spot_row = jnp.where(lane3 == s, spot[s], spot_row)
     rows3 = lax.broadcasted_iota(jnp.int32, (span, 3 * pairs), 0)
     place3 = jnp.where(rows3 == spot_row[0:1], 1.0, 0.0).astype(BF16)
-    scaled[3 * blocks] = jnp.zeros((chans, tile), BF16)
+    scaled[3 * blocks * chans // 128] = jnp.zeros((tile, 128), BF16)
 
     smalls[2].wait()
     pl.semaphore_wait(barrier, devices - 1)
@@ -122,16 +122,17 @@
     probe_left.start()
 
     contract_last = (((1,), (1,)), ((), ()))
-    sum_rows = lax.broadcasted_iota(jnp.int32, (16, tile), 0)
-    row_sum = jnp.zeros((16, tile), F32)
+    lane = lax.broadcasted_iota(jnp.int32, (tile, 128), 1)
+    ones = jnp.ones((tile, 128), BF16)
+    columns = jnp.zeros((tile, 128), F32)
     for b in range(blocks):
         loads[b].wait()
+        own = jnp.zeros((tile, 128), F32)
         for k in range(slots):
             weight = jnp.where(alive[b * slots + k], 1.0, 0.0)
-            chosen = jnp.where(sum_rows == b, weight, 0.0).astype(BF16)
-            row_sum += lax.dot_general(
-                chosen, tiles[b, k], contract_last, preferred_element_type=F32
-            )
+            own += weight * jnp.dot(tiles[b, k], ones, preferred_element_type=F32)
+        columns = jnp.where(lane == b, own, columns)
+    row_sum = columns.T
     row_inverse = 1.0 / row_sum[:blocks]
 
     def push_near(buffer, send, recv):
@@ -263,6 +264,8 @@
     probe_left.wait_recv()
     raw_right.wait_recv()
     raw_left.wait_recv()
+    quads = 128 // chans
+    pieces = []
     for side, part in ((0, 0), (1, None), (2, 1)):
         if part is None:
             inverse = root_inverse
@@ -271,14 +274,23 @@
         for b in range(blocks):
             lanes = slice(b * tile, (b + 1) * tile)
             probe = probe_ref[:, lanes] if part is None else probe_halo[part, :, lanes]
-            scaled[side * blocks + b] = (probe.astype(F32) * inverse[b : b + 1]).astype(BF16)
+            pieces.append(probe.astype(F32) * inverse[b : b + 1])
+            if len(pieces) == quads:
+                at = (side * blocks + b) // quads
+                scaled[at] = jnp.concatenate(pieces, axis=0).T.astype(BF16)
+                pieces = []
+    quad_lane = lax.broadcasted_iota(jnp.int32, (16, 128), 1) // chans
     for b in range(blocks):
-        forward = jnp.zeros((chans, tile), F32)
+        sums_up = jnp.zeros((tile, 128), F32)
         for k in range(slots):
-            forward += lax.dot_general(
-                scaled[spot[b * slots + k]], tiles[b, k], contract_last,
-                preferred_element_type=F32,
-            )
+            at = spot[b * slots + k]
+            pick = jnp.where(quad_lane == lax.rem(at, quads), 1.0, 0.0).astype(BF16)
+            chosen = scaled[at // quads] * jnp.concatenate([pick] * (tile // 16), axis=0)
+            sums_up += jnp.dot(tiles[b, k], chosen, preferred_element_type=F32)
+        turned = sums_up.T
+        forward = turned[:chans]
+        for q in range(1, quads):
+            forward += turned[q * chans : (q + 1) * chans]
         embedded[:, b * tile : (b + 1) * tile] = forward * gain[b : b + 1]
 
     for copy in part_copies:
@@ -398,7 +410,7 @@
             pltpu.VMEM((3, blocks, tile), F32),
             pltpu.VMEM((POWER, devices, 1, 128), F32),
             pltpu.VMEM((2, chans, zones), BF16),
-            pltpu.VMEM((3 * blocks + 1, chans, tile), BF16),
+            pltpu.VMEM((3 * blocks * chans // 128 + 1, tile, 128), BF16),
             pltpu.VMEM((halves, blocks * slots * chans, 128), F32),
             part, part, part, part, part,
             pltpu.VMEM((3 * chans, zones), BF16),

time: 72 us -> 71 us (0.986)
  Pallas kernels: 70.2 us -> 69.2 us
    pallas_call x1, Pallas kernels: 70.2 us -> 69.2 us  [per_device(): pl.pallas_call(functools.partial(kernel, row_axis, col_axis, group, block...]
where the time goes in v4:
time: 71 us; the launch traced here: 70.9 us
  Pallas kernels  69.2 us (97%)
  local copies, waits for them, and re-layouts  1.67 us (2%)
    pallas_call x1, Pallas kernels, per_device(): pl.pallas_call(functools.partial(kernel, row_axis, col_axis, group, block...  69.2 us
    unnamed x1, local copies, waits for them, and re-layouts  1.67 us

profile of v4, /device:TPU:0, one launch (start us, length us, event | category | flops | bytes accessed | tf_op | source)
XLA Modules:
  0.0 70.9 jit_solution(9014997713852179390)
XLA Ops:
  0.0 69.2 %embed.1 = f32[32,2048]{1,0:T(8,128)} custom-call(s32[8,8]{1,0:T(8,128)} %cols_hbm.1, s32[8]{0:T(128)} %count_hbm.1, bf16[8,8,256,256]{3,2,1,0:T(8,128)(2,1)} %tiles_hbm.1, f32[2048]{0:T(1024)} %mass_hbm.1, bf16[32,2048]{1,0:T(8,128)(2,1)} %probe_hbm.1), custom_call_target="tpu_custom_call" | custom-call | tf_op jit(solution)/shard_map/embed/pallas_call | solution.py:396
  69.2 1.7 %copy.7 = f32[32,2048]{1,0:T(8,128)} copy(f32[32,2048]{1,0:T(8,128)} %embed.1) | data formatting | bytes 524288

commit v5 on v4

--- a/solution.py
+++ b/solution.py
@@ -23,11 +23,11 @@
 
 
 def kernel(
-    row_axis, col_axis, group, blocks, slots, tile, chans,
+    row_axis, col_axis, blocks, slots, tile, chans,
     cols_hbm, count_hbm, tiles_hbm, mass_hbm, probe_hbm, out_ref,
     cols_ref, count_ref, mass_ref, probe_ref,
     tiles, place, window, landed, raw_halo, sums, probe_halo, scaled, products,
-    low, mid, up, from_left, from_right, emb_parts, embedded, near_grams, far_grams,
+    low, mid, up, from_left, from_right, emb_parts, embedded, grams,
     small_sem, load_sem, sum_send, sum_recv,
     win_send, win_recv, halo_send, halo_recv,
     probe_send, probe_recv, part_send, part_recv, gram_send, gram_recv,
@@ -39,9 +39,6 @@
     total_blocks = devices * blocks
     pairs = blocks * slots
     span = 4 * blocks
-    groups = devices // group
-    my_group = me // group
-    my_member = lax.rem(me, group)
 
     def place_of(device):
         return (device // col_axis, lax.rem(device, col_axis))
@@ -67,12 +64,6 @@
         load.start()
 
     barrier = pltpu.get_barrier_semaphore()
-
-    def near(offset):
-        return my_group * group + lax.rem(my_member + offset, group)
-
-    def far(offset):
-        return lax.rem(my_group + offset, groups) * group + my_member
 
     def greet(other):
         pl.semaphore_signal(barrier, inc=1, device_id=place_of(other), device_id_type=MESH)
@@ -134,22 +125,6 @@
         columns = jnp.where(lane == b, own, columns)
     row_sum = columns.T
     row_inverse = 1.0 / row_sum[:blocks]
-
-    def push_near(buffer, send, recv):
-        each(
-            group,
-            lambda offset: remote(
-                buffer.at[my_member], buffer.at[my_member], send, recv, near(offset)
-            ).start(),
-        )
-
-    def push_far(buffer, send, recv):
-        each(
-            groups,
-            lambda offset: remote(
-                buffer.at[my_group], buffer.at[my_group], send, recv, far(offset)
-            ).start(),
-        )
 
     def wait_all(buffer, sem, count):
         view = buffer.at[pl.ds(0, count - 1)]
@@ -312,15 +287,15 @@
     for i, j in ((2, 2), (1, 2), (2, 1), (0, 2), (2, 0), (1, 1), (0, 1), (1, 0), (0, 0)):
         gram += cross[i * chans : (i + 1) * chans, j * chans : (j + 1) * chans]
     quarters = chans // 8
-    near_grams[my_member] = jnp.concatenate(
-        [gram[q * 8 : (q + 1) * 8] for q in range(quarters)], axis=1
+    grams[me] = jnp.concatenate([gram[q * 8 : (q + 1) * 8] for q in range(quarters)], axis=1)
+    each(
+        devices,
+        lambda offset: remote(
+            grams.at[me], grams.at[me], gram_send, gram_recv, other(offset)
+        ).start(),
     )
-    push_near(near_grams, gram_send.at[0], gram_recv.at[0])
-    wait_all(near_grams, gram_recv.at[0], group)
-    far_grams[my_group] = jnp.sum(near_grams[...], axis=0)
-    push_far(far_grams, gram_send.at[1], gram_recv.at[1])
-    wait_all(far_grams, gram_recv.at[1], groups)
-    packed = jnp.sum(far_grams[...], axis=0)
+    wait_all(grams, gram_recv, devices)
+    packed = jnp.sum(grams[...], axis=0)
     gram = jnp.concatenate(
         [packed[:, q * chans : (q + 1) * chans] for q in range(quarters)], axis=0
     )
@@ -377,8 +352,7 @@
         return carry
 
     lax.fori_loop(0, POWER, drain, 0)
-    wait_all(near_grams, gram_send.at[0], group)
-    wait_all(far_grams, gram_send.at[1], groups)
+    wait_all(grams, gram_send, devices)
 
 
 def per_device(row_axis, col_axis, tile_blocks, tile_cols, tile_count, start_mass, probe_block):
@@ -389,12 +363,10 @@
     halves = tile // 128
     vmem = pl.BlockSpec(memory_space=pltpu.VMEM)
     in_hbm = pl.BlockSpec(memory_space=pltpu.HBM)
-    group = min(8, devices)
-    groups = devices // group
     dma = pltpu.SemaphoreType.DMA
     part = pltpu.VMEM((halves, chans * blocks, 128), F32)
     return pl.pallas_call(
-        functools.partial(kernel, row_axis, col_axis, group, blocks, slots, tile, chans),
+        functools.partial(kernel, row_axis, col_axis, blocks, slots, tile, chans),
         out_shape=jax.ShapeDtypeStruct((chans, zones), F32),
         in_specs=[in_hbm] * 5,
         out_specs=vmem,
@@ -415,8 +387,7 @@
             part, part, part, part, part,
             pltpu.VMEM((3 * chans, zones), BF16),
             pltpu.VMEM((chans, zones), F32),
-            pltpu.VMEM((group, 8, 128), F32),
-            pltpu.VMEM((groups, 8, 128), F32),
+            pltpu.VMEM((devices, 8, 128), F32),
             dma((4,)),
             dma((blocks,)),
             dma((POWER,)), dma((POWER,)),
@@ -424,7 +395,7 @@
             dma((2,)), dma((2,)),
             dma((2,)), dma((2,)),
             dma((2, 2)), dma((2, 2)),
-            dma((2,)), dma((2,)),
+            dma, dma,
         ],
         compiler_params=pltpu.CompilerParams(
             collective_id=0, has_side_effects=True, vmem_limit_bytes=64 * 1024 * 1024

time: 71 us -> 68.8 us (0.969)
  Pallas kernels: 69.2 us -> 67 us
    pallas_call x1, Pallas kernels: 69.2 us -> 67 us  [per_device(): pl.pallas_call(functools.partial(kernel, row_axis, col_axis, blocks, slot...]
where the time goes in v5:
time: 68.8 us; the launch traced here: 68.7 us
  Pallas kernels  67 us (97%)
  local copies, waits for them, and re-layouts  1.67 us (2%)
    pallas_call x1, Pallas kernels, per_device(): pl.pallas_call(functools.partial(kernel, row_axis, col_axis, blocks, slot...  67 us
    unnamed x1, local copies, waits for them, and re-layouts  1.67 us

profile of v5, /device:TPU:0, one launch (start us, length us, event | category | flops | bytes accessed | tf_op | source)
XLA Modules:
  0.0 68.7 jit_solution(15927055309818054243)
XLA Ops:
  0.0 67.0 %embed.1 = f32[32,2048]{1,0:T(8,128)} custom-call(s32[8,8]{1,0:T(8,128)} %cols_hbm.1, s32[8]{0:T(128)} %count_hbm.1, bf16[8,8,256,256]{3,2,1,0:T(8,128)(2,1)} %tiles_hbm.1, f32[2048]{0:T(1024)} %mass_hbm.1, bf16[32,2048]{1,0:T(8,128)(2,1)} %probe_hbm.1), custom_call_target="tpu_custom_call" | custom-call | tf_op jit(solution)/shard_map/embed/pallas_call | solution.py:368
  67.0 1.7 %copy.7 = f32[32,2048]{1,0:T(8,128)} copy(f32[32,2048]{1,0:T(8,128)} %embed.1) | data formatting | bytes 524288
